TPU v7x, 512 devices: a whole 4x8x8 slice. The times are simulated.
512 devices in a mesh: sec: 8 (over z_hi, core), tile: 64 (over x, z_lo, y).
Axes of the slice: x: 4, y: 8, z: 8 (z_hi: 4, z_lo: 2; z = z_hi * 2 + z_lo), core: 2. Of those that a mesh axis runs over, the one named last changes fastest.
Arguments:
- images: bfloat16 [16, 64, 128, 128], P('sec', 'tile'), may hold values from -6 to 6
- pair_skip: int32 [16], P('sec'), may hold values from 1 to 2
- patch_mask: int32 [16, 64, 2], P('sec', 'tile'), may hold values 0 or 1
- cotangent: bfloat16 [16, 64, 2, 128, 128], P('sec', 'tile'), may hold values from -6 to 6
- conv_weight: float32 [4, 9], replicated, may hold values from -2 to 2
- conv_bias: float32 [4], replicated, may hold values from -2 to 2
Outputs:
- feature_grad: float32 [16, 64, 4, 128, 128], P('sec', 'tile')
- weight_grad: float32 [4, 9], replicated
- bias_grad: float32 [4], replicated
Inputs may be any that keep to these rules, and one draw needn't show every extreme that they name: Section s is paired with section s + pair_skip[s]; pairs past the last section are dropped.
All inputs are finite; a program needn't handle non-finite values. No bound on the sum of `patch_mask` on one device may be relied on, other than what follows from the above.
Results may differ from a plain program's by a relative error of at most 0.0004.
Values may be sent and summed in bfloat16 or wider, within the bound.
A program may use at most 64 MiB of HBM per device.

v0:
```python
import functools

import jax
import jax.numpy as jnp
import ml_dtypes
import numpy as np
from jax import lax
from jax.experimental import pallas as pl
from jax.experimental.pallas import tpu as pltpu
from jax.sharding import PartitionSpec as P

MESH = pl.DeviceIdType.MESH
F32 = jnp.float32
BF16 = jnp.bfloat16
SIDE = 128
STEP = 64
EXT = 272
EPS = 1e-5


def dft_constants():
    index = np.arange(SIDE, dtype=np.int64)
    angle = (index[:, None] * index[None, :] % SIDE) * (2.0 * np.pi / SIDE)
    cosine, sine = np.cos(angle), np.sin(angle)
    forward = np.block([[cosine, -sine], [sine, cosine]])
    tables = []
    for table in (forward, forward.T):
        high = table.astype(ml_dtypes.bfloat16)
        low = (table - high.astype(np.float64)).astype(ml_dtypes.bfloat16)
        tables += [high, low]
    return np.stack(tables)


def split(values):
    high = values.astype(BF16)
    return high, (values - high.astype(F32)).astype(BF16)


def dot(left, right):
    return jnp.dot(left, right, preferred_element_type=F32)


def regroup(block):
    top = jnp.concatenate([block[:SIDE, :SIDE], block[SIDE:, :SIDE]], axis=1)
    low = jnp.concatenate([block[:SIDE, SIDE:], block[SIDE:, SIDE:]], axis=1)
    return jnp.concatenate([top, low], axis=0)


def total(block):
    return jnp.sum(jnp.sum(block, axis=0, keepdims=True), axis=1, keepdims=True)


def kernel(
    shape,
    images_hbm,
    cot_hbm,
    tables_hbm,
    skip_ref,
    mask_ref,
    weight_ref,
    bias_ref,
    grad_out,
    wgrad_out,
    bgrad_out,
    own_img,
    own_cot,
    tables,
    imgs,
    cots,
    away,
    flag_out,
    flag_in,
    shifts,
    feat,
    stats,
    kspec,
    cspec,
    gacc,
    acc,
    ring,
    in_sem,
    out_sem,
    send_sem,
    recv_sem,
    ring_send,
    ring_recv,
):
    n_sec, n_tile, n_low = shape
    n_high = n_tile // n_low
    sec = lax.axis_index("sec")
    tile = lax.axis_index("tile")
    low = lax.rem(tile, n_low)
    high = tile // n_low

    def sec_at(step):
        return lax.rem(sec + (step + n_sec), n_sec)

    def tile_at(step):
        return lax.rem(tile + (step + n_tile), n_tile)

    loads = [
        pltpu.make_async_copy(images_hbm, own_img, in_sem.at[0]),
        pltpu.make_async_copy(cot_hbm, own_cot, in_sem.at[1]),
        pltpu.make_async_copy(tables_hbm, tables, in_sem.at[2]),
    ]
    for load in loads:
        load.start()

    around = [(a, b) for a in (-1, 0, 1) for b in (-1, 0, 1) if (a, b) != (0, 0)]
    rings = [
        [(sec_at(d), tile) for d in range(1, n_sec)],
        [(sec, high * n_low + lax.rem(low + d, n_low)) for d in range(1, n_low)],
        [(sec, lax.rem(high + d, n_high) * n_low + low) for d in range(1, n_high)],
    ]
    barrier = pltpu.get_barrier_semaphore()
    for a, b in around:
        pl.semaphore_signal(
            barrier, inc=1, device_id=(sec_at(a), tile_at(b)), device_id_type=MESH
        )
    for group in rings:
        for device in group:
            pl.semaphore_signal(barrier, inc=1, device_id=device, device_id_type=MESH)

    loads[0].wait()
    loads[1].wait()
    skip_even = skip_ref[0]
    skip_odd = skip_ref[1]
    even_next = jnp.where(skip_even == 1, 1.0, 0.0).astype(F32)
    odd_next = jnp.where(skip_odd == 1, 1.0, 0.0).astype(F32)
    flag_out[...] = jnp.full((8, SIDE), odd_next, F32)
    for member in range(2):
        skip = (skip_even, skip_odd)[member]
        target = sec * 2 + member + skip
        inside = jnp.where(target < 2 * n_sec, 1.0, 0.0).astype(F32)
        for anchor in range(2):
            keep = mask_ref[member, anchor].astype(F32) * inside
            weighted = own_cot[member, anchor].astype(F32) * keep
            cots[1, 1 + anchor, member] = weighted.astype(BF16)
            if member == 0:
                weighted = weighted * (1.0 - even_next)
            away[anchor, member] = weighted.astype(BF16)
        imgs[1, member, STEP : STEP + SIDE] = own_img[member]
    pl.semaphore_wait(barrier, len(around) + sum(len(g) for g in rings))

    copies = {}

    def send(name, source, target, device):
        spot = len(copies)
        copy = pltpu.make_async_remote_copy(
            src_ref=source,
            dst_ref=target,
            send_sem=send_sem.at[spot],
            recv_sem=recv_sem.at[spot],
            device_id=device,
            device_id_type=MESH,
        )
        copy.start()
        copies[name] = copy

    down = own_img.at[:, pl.ds(SIDE - STEP, STEP)]
    up = own_img.at[:, pl.ds(0, EXT - SIDE - STEP)]
    top = pl.ds(0, STEP)
    bottom = pl.ds(SIDE + STEP, EXT - SIDE - STEP)
    middle = pl.ds(STEP, SIDE)
    send("down0", down, imgs.at[1, :, top], (sec, tile_at(1)))
    send("up0", up, imgs.at[1, :, bottom], (sec, tile_at(-1)))
    send("cot_t", cots.at[1, 2], cots.at[1, 0], (sec, tile_at(1)))
    send("flag", flag_out, flag_in, (sec_at(1), tile))
    for a in (1, -1):
        send(("mid", a), own_img, imgs.at[1 - a, :, middle], (sec_at(a), tile))
        send(("down", a), down, imgs.at[1 - a, :, top], (sec_at(a), tile_at(1)))
        send(("up", a), up, imgs.at[1 - a, :, bottom], (sec_at(a), tile_at(-1)))
    send("cot_s", away, cots.at[0, pl.ds(1, 2)], (sec_at(1), tile))
    send("cot_d", away.at[1], cots.at[0, 0], (sec_at(1), tile_at(1)))

    first_tile = tile == 0
    last_tile = tile == n_tile - 1
    row_keep = jnp.where(last_tile, 0.0, 1.0).astype(F32)

    loads[2].wait()

    def w_high():
        return tables[0]

    def w_low():
        return tables[1]

    def v_high():
        return tables[2]

    def v_low():
        return tables[3]

    def left_dot(first, second, block):
        hi, lo = split(block)
        return dot(
            jnp.concatenate([first, second, first], axis=1),
            jnp.concatenate([hi, hi, lo], axis=0),
        )

    def right_dot(block, first, second):
        hi, lo = split(block)
        return dot(
            jnp.concatenate([hi, lo, hi], axis=1),
            jnp.concatenate([first, first, second], axis=0),
        )

    def cot_pair(group, anchor):
        both = jnp.concatenate([cots[group, anchor, 0], cots[group, anchor, 1]], axis=0)
        rows = dot(
            jnp.concatenate([both, both], axis=1),
            jnp.concatenate([tables[0, :SIDE], tables[1, :SIDE]], axis=0),
        )
        kspec[group, anchor] = left_dot(v_high(), v_low(), regroup(rows))

    lane = lax.broadcasted_iota(jnp.int32, (EXT, SIDE), 1)
    in_one = jnp.where(lane < SIDE - 1, 1.0, 0.0).astype(F32)
    in_two = jnp.where(lane < SIDE - 2, 1.0, 0.0).astype(F32)

    def encode(slot, image, at):
        shifts[at, 0] = image
        shifts[at, 1] = pltpu.roll(image, SIDE - 1, 1) * in_one
        shifts[at, 2] = pltpu.roll(image, SIDE - 2, 1) * in_two

        def block_of(block, carry):
            start = pl.multiple_of(block * STEP, STEP)
            sums = [jnp.full((STEP, SIDE), bias_ref[c], F32) for c in range(4)]
            for u in range(3):
                for v in range(3):
                    pixels = shifts[at, v, pl.ds(start + u, STEP), :]
                    for c in range(4):
                        sums[c] = sums[c] + weight_ref[c, 3 * u + v] * pixels
            keep = jnp.where(block == 3, row_keep, 1.0)
            means, spreads = [], []
            for c in range(4):
                values = jnp.tanh(sums[c]) * keep
                feat[slot, c, pl.ds(start, STEP), :] = values
                mean = total(values) * (1.0 / (STEP * SIDE))
                away_from = values - mean
                means.append(mean)
                spreads.append(total(away_from * away_from))
            stats[slot, block] = jnp.concatenate(
                [jnp.broadcast_to(s, (1, SIDE)) for s in means + spreads], axis=0
            )
            return carry

        lax.fori_loop(0, 4, block_of, 0)

    def normal(slot, anchor, c):
        first = stats[slot, anchor, pl.ds(c, 1), :]
        second = stats[slot, anchor + 1, pl.ds(c, 1), :]
        apart = first - second
        spread = (
            stats[slot, anchor, pl.ds(4 + c, 1), :]
            + stats[slot, anchor + 1, pl.ds(4 + c, 1), :]
            + (STEP * SIDE // 2) * (apart * apart)
        )
        scale = lax.rsqrt(spread + EPS)
        start = pl.multiple_of(anchor * STEP, STEP)
        values = feat[slot, c, pl.ds(start, SIDE), :]
        return (values - 0.5 * (first + second)) * scale, scale

    def spectrum(slot, anchor):
        n = [normal(slot, anchor, c)[0] for c in range(4)]
        block = jnp.concatenate(
            [jnp.concatenate([n[0], n[1]], axis=1), jnp.concatenate([n[2], n[3]], axis=1)],
            axis=0,
        )
        rows = right_dot(block, w_high(), w_low())
        return left_dot(v_high(), v_low(), regroup(rows))

    def plain_product(k_re, k_im, spec):
        re, im = spec[:SIDE], spec[SIDE:]
        return k_re * re - k_im * im, k_re * im + k_im * re

    def conj_product(k_re, k_im, spec):
        re, im = spec[:SIDE], spec[SIDE:]
        return k_re * re + k_im * im, k_re * im - k_im * re

    def kernel_of(group, anchor, member):
        lanes = pl.ds(member * SIDE, SIDE)
        re = kspec[group, anchor, pl.ds(0, SIDE), lanes]
        im = kspec[group, anchor, pl.ds(SIDE, SIDE), lanes]
        return jnp.concatenate([re, re], axis=1), jnp.concatenate([im, im], axis=1)

    def own_cots(index, carry):
        cot_pair(1, index + 1)
        return carry

    lax.fori_loop(0, 2, own_cots, 0)
    gacc[...] = jnp.zeros_like(gacc)
    acc[...] = jnp.zeros_like(acc)
    for name in ("down0", "up0", "cot_t"):
        copies[name].wait_recv()

    @pl.when(first_tile)
    def _():
        cots[1, 0] = jnp.zeros((2, SIDE, SIDE), BF16)

    @pl.when(last_tile)
    def _():
        imgs[1, :, bottom] = jnp.zeros((2, EXT - SIDE - STEP, SIDE), BF16)

    def own_sections(member, carry):
        encode(member, imgs[1, member].astype(F32), member)
        return carry

    lax.fori_loop(0, 2, own_sections, 0)
    cot_pair(1, 0)

    def own_spectra(anchor, carry):
        cspec[anchor] = spectrum(0, anchor)
        return carry

    lax.fori_loop(0, 3, own_spectra, 0)

    for name in copies:
        if name not in ("down0", "up0", "cot_t"):
            copies[name].wait_recv()

    @pl.when(last_tile)
    def _():
        for side in (0, 2):
            imgs[side, :, bottom] = jnp.zeros((2, EXT - SIDE - STEP, SIDE), BF16)

    @pl.when(first_tile)
    def _():
        cots[0, 0] = jnp.zeros((2, SIDE, SIDE), BF16)

    @pl.when(sec == 0)
    def _():
        cots[0] = jnp.zeros((3, 2, SIDE, SIDE), BF16)

    def prior_sections(member, carry):
        encode(2 + member, imgs[0, member].astype(F32), 2)
        return carry

    lax.fori_loop(0, 2, prior_sections, 0)
    ahead = imgs[2, 0].astype(F32)
    encode(4, even_next * imgs[1, 1].astype(F32) + (1.0 - even_next) * ahead, 2)
    encode(5, odd_next * imgs[2, 0].astype(F32) + (1.0 - odd_next) * imgs[2, 1].astype(F32), 2)

    def anchors(anchor, carry):
        cot_pair(0, anchor)
        came_next = flag_in[0:1, 0:1]
        k_re, k_im = kernel_of(0, anchor, 1)
        last_re, last_im = plain_product(k_re, k_im, spectrum(3, anchor))
        g_re = came_next * last_re
        g_im = came_next * last_im
        h_re = last_re - g_re
        h_im = last_im - g_im
        k_re, k_im = kernel_of(0, anchor, 0)
        p_re, p_im = plain_product(k_re, k_im, spectrum(2, anchor))
        g_re, g_im = g_re + p_re, g_im + p_im
        k_re, k_im = kernel_of(1, anchor, 0)
        p_re, p_im = conj_product(k_re, k_im, spectrum(4, anchor))
        g_re, g_im = g_re + p_re, g_im + p_im
        p_re, p_im = plain_product(k_re, k_im, cspec[anchor])
        h_re, h_im = h_re + even_next * p_re, h_im + even_next * p_im
        k_re, k_im = kernel_of(1, anchor, 1)
        p_re, p_im = conj_product(k_re, k_im, spectrum(5, anchor))
        h_re, h_im = h_re + p_re, h_im + p_im
        for member, (re, im) in enumerate(((g_re, g_im), (h_re, h_im))):
            half = left_dot(w_high(), w_low(), jnp.concatenate([re, im], axis=0))
            back = right_dot(regroup(half), v_high(), v_low())
            for c in range(4):
                q, part = c // 2, c % 2
                slope = back[q * SIDE : (q + 1) * SIDE, part * SIDE : (part + 1) * SIDE]
                slope = slope * (0.25 / (SIDE * SIDE))
                unit, scale = normal(member, anchor, c)
                along = total(slope * unit)
                start = pl.multiple_of(anchor * STEP, STEP)
                gacc[member, c, pl.ds(start, SIDE), :] += scale * (slope - unit * along)
        return carry

    lax.fori_loop(0, 3, anchors, 0)

    results = [
        pltpu.make_async_copy(
            gacc.at[member, :, middle], grad_out.at[member], out_sem.at[member]
        )
        for member in range(2)
    ]
    for result in results:
        result.start()

    def weight_steps(index, carry):
        member = index // 2
        start = pl.multiple_of(STEP + lax.rem(index, 2) * STEP, STEP)
        slopes = []
        for c in range(4):
            values = feat[member, c, pl.ds(start, STEP), :]
            slope = gacc[member, c, pl.ds(start, STEP), :] * (1.0 - values * values)
            slopes.append(slope)
            acc[10 * c + 9] += jnp.sum(slope.reshape(STEP // 8, 8, SIDE), axis=0)
        for u in range(3):
            for v in range(3):
                pixels = shifts[member, v, pl.ds(start + u, STEP), :]
                for c in range(4):
                    part = slopes[c] * pixels
                    acc[10 * c + 3 * u + v] += jnp.sum(part.reshape(STEP // 8, 8, SIDE), axis=0)
        return carry

    lax.fori_loop(0, 4, weight_steps, 0)
    sub8 = lax.broadcasted_iota(jnp.int32, (8, SIDE), 0)
    lane8 = lax.broadcasted_iota(jnp.int32, (8, SIDE), 1)
    mine = jnp.zeros((8, SIDE), F32)
    for tap in range(10):
        for c in range(4):
            spot = (c, tap) if tap < 9 else (4, c)
            here = jnp.logical_and(sub8 == spot[0], lane8 == spot[1])
            mine = mine + jnp.where(here, total(acc[10 * c + tap]), 0.0)

    spots = (sec, low, high)
    sizes = (n_sec, n_low, n_high)
    for stage in range(3):
        spot = spots[stage]
        ring[stage, spot] = mine
        moves = []
        for d in range(1, sizes[stage]):
            copy = pltpu.make_async_remote_copy(
                src_ref=ring.at[stage, spot],
                dst_ref=ring.at[stage, spot],
                send_sem=ring_send.at[stage, d],
                recv_sem=ring_recv.at[stage, d],
                device_id=rings[stage][d - 1],
                device_id_type=MESH,
            )
            copy.start()
            moves.append(copy)
        for copy in moves:
            copy.wait_recv()
        mine = jnp.sum(ring[stage, 0 : sizes[stage]], axis=0)
        for copy in moves:
            copy.wait_send()
    wgrad_out[...] = mine[0:4, 0:9]
    bgrad_out[...] = mine[4:5, 0:4]
    for copy in copies.values():
        copy.wait_send()
    for result in results:
        result.wait()


def on_device(shape, images, pair_skip, patch_mask, cotangent, conv_weight, conv_bias):
    hbm = pl.BlockSpec(memory_space=pl.ANY)
    smem = pl.BlockSpec(memory_space=pltpu.SMEM)
    vmem = pl.BlockSpec(memory_space=pltpu.VMEM)
    wide = max(shape[0], shape[2], shape[1] // shape[2])
    grad, weight_grad, bias_grad = pl.pallas_call(
        functools.partial(kernel, shape),
        out_shape=(
            jax.ShapeDtypeStruct((2, 4, SIDE, SIDE), F32),
            jax.ShapeDtypeStruct((4, 9), F32),
            jax.ShapeDtypeStruct((1, 4), F32),
        ),
        in_specs=[hbm, hbm, hbm, smem, smem, smem, smem],
        out_specs=(hbm, vmem, vmem),
        scratch_shapes=[
            pltpu.VMEM((2, SIDE, SIDE), BF16),
            pltpu.VMEM((2, 2, SIDE, SIDE), BF16),
            pltpu.VMEM((4, 2 * SIDE, 2 * SIDE), BF16),
            pltpu.VMEM((3, 2, EXT, SIDE), BF16),
            pltpu.VMEM((2, 3, 2, SIDE, SIDE), BF16),
            pltpu.VMEM((2, 2, SIDE, SIDE), BF16),
            pltpu.VMEM((8, SIDE), F32),
            pltpu.VMEM((8, SIDE), F32),
            pltpu.VMEM((3, 3, EXT, SIDE), F32),
            pltpu.VMEM((6, 4, 4 * STEP, SIDE), F32),
            pltpu.VMEM((6, 4, 8, SIDE), F32),
            pltpu.VMEM((2, 3, 2 * SIDE, 2 * SIDE), F32),
            pltpu.VMEM((3, 2 * SIDE, 2 * SIDE), F32),
            pltpu.VMEM((2, 4, 4 * STEP, SIDE), F32),
            pltpu.VMEM((40, 8, SIDE), F32),
            pltpu.VMEM((3, wide, 8, SIDE), F32),
            pltpu.SemaphoreType.DMA((3,)),
            pltpu.SemaphoreType.DMA((2,)),
            pltpu.SemaphoreType.DMA((12,)),
            pltpu.SemaphoreType.DMA((12,)),
            pltpu.SemaphoreType.DMA((3, wide)),
            pltpu.SemaphoreType.DMA((3, wide)),
        ],
        compiler_params=pltpu.CompilerParams(
            collective_id=0, has_side_effects=True, vmem_limit_bytes=48 * 1024 * 1024
        ),
    )(
        images[:, 0],
        cotangent[:, 0],
        jnp.asarray(dft_constants()),
        pair_skip,
        patch_mask[:, 0],
        conv_weight,
        conv_bias,
    )
    return grad[:, None], weight_grad, bias_grad[0]


def solution(mesh):
    n_sec, n_tile = mesh.shape["sec"], mesh.shape["tile"]
    n_low = 8 if n_tile % 8 == 0 else 2
    return jax.shard_map(
        functools.partial(on_device, (n_sec, n_tile, n_low)),
        mesh=mesh,
        in_specs=(
            P("sec", "tile", None, None),
            P("sec"),
            P("sec", "tile", None),
            P("sec", "tile", None, None, None),
            P(),
            P(),
        ),
        out_specs=(P("sec", "tile", None, None, None), P(), P()),
        check_vma=False,
    )
```

profile of v0, /device:TPU:1, one launch (start us, length us, event | category | flops | bytes accessed | tf_op | source)
XLA Modules:
  0.0 59.0 jit_solution(4702639968808733687)
XLA Ops:
  0.6 0.0 copy-start.6
  0.6 0.0 copy-start.3
  0.7 0.0 copy-start.4
  0.7 0.0 copy-start.5
  0.7 0.6 %copy-done.6 = f32[4]{0:T(128)S(1)} copy-done((f32[4]{0:T(128)S(1)}, f32[4]{0:T(128)}, u32[]{:S(2)}) %copy-start.6) | copy-done | bytes 40
  1.3 0.0 copy-done.3
  1.3 0.0 copy-done.4
  1.3 0.0 copy-done.5
  1.3 0.0 copy-start
  1.3 1.0 %copy-done = bf16[4,256,256]{2,1,0:T(8,128)(2,1)S(1)} copy-done((bf16[4,256,256]{2,1,0:T(8,128)(2,1)S(1)}, bf16[4,256,256]{2,1,0:T(8,128)(2,1)}, u32[]{:S(2)}) %copy-start) | copy-done | bytes 524312
  2.4 0.0 copy-start.1
  2.4 0.9 %copy-done.1 = bf16[2,1,2,128,128]{4,3,2,1,0:T(8,128)(2,1)S(1)} copy-done((bf16[2,1,2,128,128]{4,3,2,1,0:T(8,128)(2,1)S(1)}, bf16[2,1,2,128,128]{4,3,2,1,0:T(8,128)(2,1)}, u32[]{:S(2)}) %copy-start.1) | copy-done | bytes 131096
  3.3 0.0 copy-start.2
  3.3 0.8 %copy-done.2 = bf16[2,1,128,128]{3,2,1,0:T(8,128)(2,1)S(1)} copy-done((bf16[2,1,128,128]{3,2,1,0:T(8,128)(2,1)S(1)}, bf16[2,1,128,128]{3,2,1,0:T(8,128)(2,1)}, u32[]{:S(2)}) %copy-start.2) | copy-done | bytes 65560
  4.1 53.0 %shard_map.94 = (f32[2,4,128,128]{3,2,1,0:T(8,128)S(1)}, f32[4,9]{1,0:T(4,128)S(1)}, f32[1,4]{1,0:T(1,128)S(1)}) custom-call(bf16[2,128,128]{2,1,0:T(8,128)(2,1)S(1)} %bitcast.9, bf16[2,2,128,128]{3,2,1,0:T(8,128)(2,1)S(1)} %bitcast.8, bf16[4,256,256]{2,1,0:T(8,128)(2,1)S(1)} %copy-done, s32[2]{0:T(128)S(1)} %copy-done.5, s32[2,2]{1,0:T(2,128)S(1)} %bitcast.10, ...), custom_call_target="tpu_custom_call" | custom-call | tf_op jit(solution)/shard_map/pallas_call | solution.py:449
  57.1 0.8 %copy.14 = f32[2,1,4,128,128]{4,3,2,1,0:T(8,128)} copy(f32[2,1,4,128,128]{4,3,2,1,0:T(8,128)S(1)} %bitcast.7) | data formatting | bytes 1048576
  57.9 0.6 copy.15
  58.5 0.5 copy.16
Async XLA Ops:
  0.6 0.7 %copy-start.6 = (f32[4]{0:T(128)S(1)}, f32[4]{0:T(128)}, u32[]{:S(2)}) copy-start(f32[4]{0:T(128)} %bias_ref.1) | copy-start | bytes 52
  0.6 0.7 %copy-start.3 = (f32[4,9]{1,0:T(4,128)S(1)}, f32[4,9]{1,0:T(4,128)}, u32[]{:S(2)}) copy-start(f32[4,9]{1,0:T(4,128)} %weight_ref.1) | copy-start | bytes 436
  0.7 0.7 %copy-start.4 = (s32[2,1,2]{2,1,0:T(1,128)S(1)}, s32[2,1,2]{2,1,0:T(1,128)}, u32[]{:S(2)}) copy-start(s32[2,1,2]{2,1,0:T(1,128)} %param.9) | copy-start | bytes 52
  0.7 0.7 %copy-start.5 = (s32[2]{0:T(128)S(1)}, s32[2]{0:T(128)}, u32[]{:S(2)}) copy-start(s32[2]{0:T(128)} %skip_ref.1) | copy-start | bytes 28
  1.3 1.0 %copy-start = (bf16[4,256,256]{2,1,0:T(8,128)(2,1)S(1)}, bf16[4,256,256]{2,1,0:T(8,128)(2,1)}, u32[]{:S(2)}) copy-start(bf16[4,256,256]{2,1,0:T(8,128)(2,1)} %constant.2.clone.tables_hbm) | copy-start | bytes 1572868
  2.4 0.9 %copy-start.1 = (bf16[2,1,2,128,128]{4,3,2,1,0:T(8,128)(2,1)S(1)}, bf16[2,1,2,128,128]{4,3,2,1,0:T(8,128)(2,1)}, u32[]{:S(2)}) copy-start(bf16[2,1,2,128,128]{4,3,2,1,0:T(8,128)(2,1)} %param.10) | copy-start | bytes 393220
  3.3 0.8 %copy-start.2 = (bf16[2,1,128,128]{3,2,1,0:T(8,128)(2,1)S(1)}, bf16[2,1,128,128]{3,2,1,0:T(8,128)(2,1)}, u32[]{:S(2)}) copy-start(bf16[2,1,128,128]{3,2,1,0:T(8,128)(2,1)} %param.7) | copy-start | bytes 196612
where the time goes:
time: 59.2 us; the launch traced here: 59 us
  Pallas kernels  53 us (90%)
  local copies, waits for them, and re-layouts  5.35 us (9%)
  between operations  0.68 us (1%)
    pallas_call x1, Pallas kernels, on_device(): pl.pallas_call(functools.partial(kernel, shape), out_shape=(jax.ShapeDtyp...  53 us
    unnamed x17, local copies, waits for them, and re-layouts  5.35 us

commit v1 on v0

v1 whole, which is shorter than its diff:
```python
import functools

import jax
import jax.numpy as jnp
import ml_dtypes
import numpy as np
from jax import lax
from jax.experimental import pallas as pl
from jax.experimental.pallas import tpu as pltpu
from jax.sharding import PartitionSpec as P

MESH = pl.DeviceIdType.MESH
F32 = jnp.float32
BF16 = jnp.bfloat16
SIDE = 128
STEP = 64
EXT = 272
EPS = 1e-5


def dft_constants():
    index = np.arange(SIDE, dtype=np.int64)
    angle = (index[:, None] * index[None, :] % SIDE) * (2.0 * np.pi / SIDE)
    cosine, sine = np.cos(angle), np.sin(angle)
    along = np.block([[cosine, -sine], [sine, cosine]])
    def parts(table):
        high = table.astype(ml_dtypes.bfloat16)
        low = (table - high.astype(np.float64)).astype(ml_dtypes.bfloat16)
        return [high, low]

    return np.stack(parts(along) + parts(along.T))


def split(values):
    high = values.astype(BF16)
    return high, (values - high.astype(F32)).astype(BF16)


def dot(left, right):
    return jnp.dot(left, right, preferred_element_type=F32)


def regroup(block):
    top = jnp.concatenate([block[:SIDE, :SIDE], block[SIDE:, :SIDE]], axis=1)
    low = jnp.concatenate([block[:SIDE, SIDE:], block[SIDE:, SIDE:]], axis=1)
    return jnp.concatenate([top, low], axis=0)


def total(block):
    return jnp.sum(jnp.sum(block, axis=0, keepdims=True), axis=1, keepdims=True)


def kernel(
    shape,
    images_hbm,
    cot_hbm,
    tables_hbm,
    skip_ref,
    mask_ref,
    weight_ref,
    bias_ref,
    grad_out,
    sums_out,
    own_cot,
    tables,
    imgs,
    cots,
    flag_out,
    flag_in,
    band,
    pixels,
    shifts,
    feat,
    stats,
    kspec,
    gspec,
    aspec,
    gacc,
    acc,
    ring,
    in_sem,
    out_sem,
    send_sem,
    recv_sem,
    ring_send,
    ring_recv,
):
    n_sec, n_x, n_z, n_y = shape
    n_tile = n_x * n_z * n_y
    sec = lax.axis_index("sec")
    tile = lax.axis_index("tile")
    at_x = tile // (n_z * n_y)
    at_z = lax.rem(tile // n_y, n_z)
    at_y = lax.rem(tile, n_y)

    def sec_at(step):
        return lax.rem(sec + (step + n_sec), n_sec)

    def tile_at(step):
        return lax.rem(tile + (step + n_tile), n_tile)

    around = [(1, 0), (-1, 0), (0, 1), (0, -1)]
    spots = (sec * n_z + at_z, at_x * n_y + at_y)
    sizes = (n_sec * n_z, n_x * n_y)

    def in_ring(stage, step):
        there = lax.rem(spots[stage] + step, sizes[stage])
        if stage == 0:
            return there // n_z, (at_x * n_z + lax.rem(there, n_z)) * n_y + at_y
        return sec, (there // n_y * n_z + at_z) * n_y + lax.rem(there, n_y)

    rings = [[in_ring(stage, d) for d in range(1, sizes[stage])] for stage in range(2)]
    barrier = pltpu.get_barrier_semaphore()
    for a, b in around:
        pl.semaphore_signal(
            barrier, inc=1, device_id=(sec_at(a), tile_at(b)), device_id_type=MESH
        )
    for group in rings:
        for device in group:
            pl.semaphore_signal(barrier, inc=1, device_id=device, device_id_type=MESH)

    middle = pl.ds(STEP, SIDE)
    loads = [
        pltpu.make_async_copy(images_hbm, imgs.at[1, :, middle], in_sem.at[0]),
        pltpu.make_async_copy(cot_hbm, own_cot, in_sem.at[1]),
        pltpu.make_async_copy(tables_hbm, tables, in_sem.at[2]),
    ]
    for load in loads:
        load.start()
    pl.semaphore_wait(barrier, len(around) + sum(len(g) for g in rings))

    copies = {}

    def send(name, source, target, device):
        spot = len(copies)
        copy = pltpu.make_async_remote_copy(
            src_ref=source,
            dst_ref=target,
            send_sem=send_sem.at[spot],
            recv_sem=recv_sem.at[spot],
            device_id=device,
            device_id_type=MESH,
        )
        copy.start()
        copies[name] = copy

    down = images_hbm.at[:, pl.ds(SIDE - STEP, STEP)]
    up = images_hbm.at[:, pl.ds(0, EXT - SIDE - STEP)]
    top = pl.ds(0, STEP)
    bottom = pl.ds(SIDE + STEP, EXT - SIDE - STEP)
    send("down0", down, imgs.at[1, :, top], (sec, tile_at(1)))
    send("up0", up, imgs.at[1, :, bottom], (sec, tile_at(-1)))
    for a in (1, -1):
        send(("mid", a), images_hbm, imgs.at[1 - a, :, middle], (sec_at(a), tile))

    skip_even = skip_ref[0]
    skip_odd = skip_ref[1]
    even_next = jnp.where(skip_even == 1, 1.0, 0.0).astype(F32)
    odd_next = jnp.where(skip_odd == 1, 1.0, 0.0).astype(F32)
    flag_out[0:1] = jnp.full((1, SIDE), odd_next, F32)
    flag_out[1:2] = jnp.full((1, SIDE), 1.0 - even_next, F32)
    loads[1].wait()
    for member in range(2):
        skip = (skip_even, skip_odd)[member]
        target = sec * 2 + member + skip
        inside = jnp.where(target < 2 * n_sec, 1.0, 0.0).astype(F32)
        for anchor in range(2):
            keep = mask_ref[member, anchor].astype(F32) * inside
            weighted = own_cot[member, anchor].astype(F32) * keep
            cots[1, 1 + anchor, member] = weighted.astype(BF16)
    send("cot_t", cots.at[1, 2], cots.at[1, 0], (sec, tile_at(1)))
    send("flag", flag_out, flag_in, (sec_at(1), tile))
    send("cot_s", cots.at[1, pl.ds(1, 2)], cots.at[0, pl.ds(1, 2)], (sec_at(1), tile))

    first_tile = tile == 0
    last_tile = tile == n_tile - 1
    row_keep = jnp.where(last_tile, 0.0, 1.0).astype(F32)

    def w_high():
        return tables[0]

    def w_low():
        return tables[1]

    def v_high():
        return tables[2]

    def v_low():
        return tables[3]

    def left_dot(first, second, block):
        hi, lo = split(block)
        return dot(
            jnp.concatenate([first, second, first], axis=1),
            jnp.concatenate([hi, hi, lo], axis=0),
        )

    def right_dot(block, first, second):
        hi, lo = split(block)
        return dot(
            jnp.concatenate([hi, lo, hi], axis=1),
            jnp.concatenate([first, first, second], axis=0),
        )

    def cot_pair(group, anchor):
        both = jnp.concatenate([cots[group, anchor, 0], cots[group, anchor, 1]], axis=0)
        rows = dot(
            jnp.concatenate([both, both], axis=1),
            jnp.concatenate([tables[0, :SIDE], tables[1, :SIDE]], axis=0),
        )
        kspec[group, anchor] = left_dot(v_high(), v_low(), regroup(rows))

    apart = lax.broadcasted_iota(jnp.int32, (SIDE, SIDE), 0) - lax.broadcasted_iota(
        jnp.int32, (SIDE, SIDE), 1
    )

    def band_rows(u, carry):
        for c in range(4):
            table = jnp.zeros((SIDE, SIDE), F32)
            for v in range(3):
                table = jnp.where(apart == v, weight_ref[c, 3 * u + v], table)
            hi, lo = split(table)
            lanes = pl.ds(c * SIDE, SIDE)
            band[pl.ds(pl.multiple_of(u * SIDE, SIDE), SIDE), lanes] = hi
            band[pl.ds(pl.multiple_of((3 + u) * SIDE, SIDE), SIDE), lanes] = lo
        return carry

    lane = lax.broadcasted_iota(jnp.int32, (EXT, SIDE), 1)
    in_one = jnp.where(lane < SIDE - 1, 1.0, 0.0).astype(F32)
    in_two = jnp.where(lane < SIDE - 2, 1.0, 0.0).astype(F32)

    def encode(slot, image):
        rows = [image[u : u + 4 * STEP, :].astype(BF16) for u in range(3)]
        sums = dot(jnp.concatenate(rows + rows, axis=1), band[...])
        means, spreads = [], []
        for c in range(4):
            values = jnp.tanh(sums[:, c * SIDE : (c + 1) * SIDE] + bias_ref[c])
            blocks = [values[b * STEP : (b + 1) * STEP] for b in range(4)]
            blocks[3] = blocks[3] * row_keep
            for b in range(4):
                feat[slot, c, b * STEP : (b + 1) * STEP] = blocks[b]
                mean = total(blocks[b]) * (1.0 / (STEP * SIDE))
                means.append(mean)
                off = blocks[b] - mean
                spreads.append(total(off * off))
        for b in range(4):
            stats[slot, b] = jnp.concatenate(
                [jnp.broadcast_to(s, (1, SIDE)) for s in means[b::4] + spreads[b::4]], axis=0
            )

    def normal(slot, anchor, c):
        first = stats[slot, anchor, pl.ds(c, 1), :]
        second = stats[slot, anchor + 1, pl.ds(c, 1), :]
        apart = first - second
        spread = (
            stats[slot, anchor, pl.ds(4 + c, 1), :]
            + stats[slot, anchor + 1, pl.ds(4 + c, 1), :]
            + (STEP * SIDE // 2) * (apart * apart)
        )
        scale = lax.rsqrt(spread + EPS)
        start = anchor * STEP
        values = feat[slot, c, pl.ds(start, SIDE), :]
        return (values - 0.5 * (first + second)) * scale, scale

    def spectrum(slot, anchor):
        n = [normal(slot, anchor, c)[0] for c in range(4)]
        block = jnp.concatenate(
            [jnp.concatenate([n[0], n[1]], axis=1), jnp.concatenate([n[2], n[3]], axis=1)],
            axis=0,
        )
        rows = right_dot(block, w_high(), w_low())
        return left_dot(v_high(), v_low(), regroup(rows))

    def plain_product(k_re, k_im, spec):
        re, im = spec[:SIDE], spec[SIDE:]
        return k_re * re - k_im * im, k_re * im + k_im * re

    def conj_product(k_re, k_im, spec):
        re, im = spec[:SIDE], spec[SIDE:]
        return k_re * re + k_im * im, k_re * im - k_im * re

    def kernel_of(group, anchor, member):
        lanes = pl.ds(member * SIDE, SIDE)
        re = kspec[group, anchor, pl.ds(0, SIDE), lanes]
        im = kspec[group, anchor, pl.ds(SIDE, SIDE), lanes]
        return jnp.concatenate([re, re], axis=1), jnp.concatenate([im, im], axis=1)

    lax.fori_loop(0, 3, band_rows, 0)
    loads[2].wait()
    loads[0].wait()
    def own_cots(index, carry):
        cot_pair(1, index + 1)
        return carry

    lax.fori_loop(0, 2, own_cots, 0)
    gacc[...] = jnp.zeros_like(gacc)
    acc[...] = jnp.zeros_like(acc)
    for name in ("down0", "up0", "cot_t"):
        copies[name].wait_recv()

    @pl.when(first_tile)
    def _():
        cots[1, 0] = jnp.zeros((2, SIDE, SIDE), BF16)

    @pl.when(last_tile)
    def _():
        imgs[1, :, bottom] = jnp.zeros((2, EXT - SIDE - STEP, SIDE), BF16)

    for a in (1, -1):
        for name, rows in (("down", top), ("up", bottom)):
            send((name, a), imgs.at[1, :, rows], imgs.at[1 - a, :, rows], (sec_at(a), tile))
    send("cot_d", cots.at[1, 0], cots.at[0, 0], (sec_at(1), tile))

    def own_sections(member, carry):
        image = imgs[1, member].astype(F32)
        shifts[member, 0] = image
        shifts[member, 1] = pltpu.roll(image, SIDE - 1, 1) * in_one
        shifts[member, 2] = pltpu.roll(image, SIDE - 2, 1) * in_two
        encode(member, shifts.at[member, 0])
        return carry

    lax.fori_loop(0, 2, own_sections, 0)
    cot_pair(1, 0)

    def own_spectra(anchor, carry):
        k_re, k_im = kernel_of(1, anchor, 0)
        re, im = plain_product(k_re, k_im, spectrum(0, anchor))
        gspec[anchor, 0:SIDE] = even_next * re
        gspec[anchor, SIDE:] = even_next * im
        return carry

    lax.fori_loop(0, 3, own_spectra, 0)

    def wait_images(a):
        for name in ("mid", "down", "up"):
            copies[name, a].wait_recv()

    def step(phase, carry):
        before = lax.rem(sec + phase, 2) == 1

        @pl.when(before)
        def _():
            wait_images(1)
            pixels[0] = imgs[0, 0].astype(F32)
            pixels[1] = imgs[0, 1].astype(F32)

        @pl.when(jnp.logical_not(before))
        def _():
            wait_images(-1)
            ahead = imgs[2, 0].astype(F32)
            pixels[2] = even_next * shifts[1, 0] + (1.0 - even_next) * ahead
            pixels[3] = odd_next * ahead + (1.0 - odd_next) * imgs[2, 1].astype(F32)

        base = 2 * lax.rem(sec + phase + 1, 2)
        for i in range(2):
            encode(2 + base + i, pixels.at[base + i])
        for anchor in range(3):
            for i in range(2):
                aspec[base + i, anchor] = spectrum(2 + base + i, anchor)
        return carry

    lax.fori_loop(0, 2, step, 0)

    for name in ("flag", "cot_s", "cot_d"):
        copies[name].wait_recv()

    @pl.when(sec == 0)
    def _():
        cots[0] = jnp.zeros((3, 2, SIDE, SIDE), BF16)

    def finish(anchor):
        cot_pair(0, anchor)
        came_next = flag_in[0:1, 0:1]
        came_after = flag_in[1:2, 0:1]
        k_re, k_im = kernel_of(0, anchor, 1)
        last_re, last_im = plain_product(k_re, k_im, aspec[1, anchor])
        k_re, k_im = kernel_of(0, anchor, 0)
        p_re, p_im = plain_product(came_after * k_re, came_after * k_im, aspec[0, anchor])
        g_re = p_re + came_next * last_re
        g_im = p_im + came_next * last_im
        h_re = gspec[anchor, 0:SIDE] + (1.0 - came_next) * last_re
        h_im = gspec[anchor, SIDE:] + (1.0 - came_next) * last_im
        k_re, k_im = kernel_of(1, anchor, 0)
        p_re, p_im = conj_product(k_re, k_im, aspec[2, anchor])
        g_re, g_im = g_re + p_re, g_im + p_im
        k_re, k_im = kernel_of(1, anchor, 1)
        p_re, p_im = conj_product(k_re, k_im, aspec[3, anchor])
        h_re, h_im = h_re + p_re, h_im + p_im
        for member, (re, im) in enumerate(((g_re, g_im), (h_re, h_im))):
            half = left_dot(w_high(), w_low(), jnp.concatenate([re, im], axis=0))
            back = right_dot(regroup(half), v_high(), v_low())
            for c in range(4):
                q, part = c // 2, c % 2
                slope = back[q * SIDE : (q + 1) * SIDE, part * SIDE : (part + 1) * SIDE]
                slope = slope * (0.25 / (SIDE * SIDE))
                unit, scale = normal(member, anchor, c)
                along = total(slope * unit)
                start = anchor * STEP
                gacc[member, c, pl.ds(start, SIDE), :] += scale * (slope - unit * along)

    for anchor in range(3):
        finish(anchor)

    results = [
        pltpu.make_async_copy(
            gacc.at[member, :, middle], grad_out.at[member], out_sem.at[member]
        )
        for member in range(2)
    ]
    for result in results:
        result.start()

    def weight_steps(index, carry):
        member = index // 2
        start = pl.multiple_of(STEP + lax.rem(index, 2) * STEP, STEP)
        slopes = []
        for c in range(4):
            values = feat[member, c, pl.ds(start, STEP), :]
            slope = gacc[member, c, pl.ds(start, STEP), :] * (1.0 - values * values)
            slopes.append(slope)
            acc[10 * c + 9] += jnp.sum(slope.reshape(STEP // 8, 8, SIDE), axis=0)
        for u in range(3):
            for v in range(3):
                shifted = shifts[member, v, pl.ds(start + u, STEP), :]
                for c in range(4):
                    part = slopes[c] * shifted
                    acc[10 * c + 3 * u + v] += jnp.sum(part.reshape(STEP // 8, 8, SIDE), axis=0)
        return carry

    lax.fori_loop(0, 4, weight_steps, 0)
    place = lax.broadcasted_iota(jnp.int32, (1, SIDE), 1)
    mine = jnp.zeros((1, SIDE), F32)
    for index in range(40):
        mine = mine + jnp.where(place == index, total(acc[index]), 0.0)
    for stage in range(2):
        spot = spots[stage]
        ring[stage, spot] = mine
        moves = []
        for d in range(1, sizes[stage]):
            copy = pltpu.make_async_remote_copy(
                src_ref=ring.at[stage, spot],
                dst_ref=ring.at[stage, spot],
                send_sem=ring_send.at[stage, d],
                recv_sem=ring_recv.at[stage, d],
                device_id=rings[stage][d - 1],
                device_id_type=MESH,
            )
            copy.start()
            moves.append(copy)
        for copy in moves:
            copy.wait_recv()
        mine = jnp.sum(ring[stage, 0 : sizes[stage]], axis=0)
        for copy in moves:
            copy.wait_send()
    sums_out[...] = mine
    for copy in copies.values():
        copy.wait_send()
    for result in results:
        result.wait()


def deliver(grad_ref, sums_ref, grad_out, wgrad_out, bgrad_out):
    grad_out[...] = grad_ref[...]
    sums = jnp.broadcast_to(sums_ref[...], (8, SIDE))
    row = lax.broadcasted_iota(jnp.int32, (8, SIDE), 0)
    place = lax.broadcasted_iota(jnp.int32, (8, SIDE), 1)
    taps = jnp.zeros((8, SIDE), F32)
    biases = jnp.zeros((8, SIDE), F32)
    for c in range(4):
        moved = pltpu.roll(sums, (SIDE - 10 * c) % SIDE, 1)
        taps = jnp.where(row == c, moved, taps)
        moved = pltpu.roll(sums, (SIDE - 10 * c - 9 + c) % SIDE, 1)
        biases = jnp.where(place == c, moved, biases)
    wgrad_out[...] = taps[0:4, 0:9]
    bgrad_out[...] = biases[0:1, 0:4]


def on_device(shape, images, pair_skip, patch_mask, cotangent, conv_weight, conv_bias):
    hbm = pl.BlockSpec(memory_space=pl.ANY)
    smem = pl.BlockSpec(memory_space=pltpu.SMEM)
    vmem = pl.BlockSpec(memory_space=pltpu.VMEM)
    wide = max(shape[0] * shape[2], shape[1] * shape[3])
    held = pl.BlockSpec(memory_space=pltpu.HBM)
    member = pl.BlockSpec((1, 4, SIDE, SIDE), lambda i: (i, 0, 0, 0))
    grad, sums = pl.pallas_call(
        functools.partial(kernel, shape),
        out_shape=(
            jax.ShapeDtypeStruct((2, 4, SIDE, SIDE), F32),
            jax.ShapeDtypeStruct((1, SIDE), F32),
        ),
        in_specs=[held, held, held, smem, smem, smem, smem],
        out_specs=(hbm, vmem),
        scratch_shapes=[
            pltpu.VMEM((2, 2, SIDE, SIDE), BF16),
            pltpu.VMEM((4, 2 * SIDE, 2 * SIDE), BF16),
            pltpu.VMEM((3, 2, EXT, SIDE), BF16),
            pltpu.VMEM((2, 3, 2, SIDE, SIDE), BF16),
            pltpu.VMEM((8, SIDE), F32),
            pltpu.VMEM((8, SIDE), F32),
            pltpu.VMEM((6 * SIDE, 4 * SIDE), BF16),
            pltpu.VMEM((4, EXT, SIDE), F32),
            pltpu.VMEM((2, 3, EXT, SIDE), F32),
            pltpu.VMEM((6, 4, 4 * STEP, SIDE), F32),
            pltpu.VMEM((6, 4, 8, SIDE), F32),
            pltpu.VMEM((2, 3, 2 * SIDE, 2 * SIDE), F32),
            pltpu.VMEM((3, 2 * SIDE, 2 * SIDE), F32),
            pltpu.VMEM((4, 3, 2 * SIDE, 2 * SIDE), F32),
            pltpu.VMEM((2, 4, 4 * STEP, SIDE), F32),
            pltpu.VMEM((40, 8, SIDE), F32),
            pltpu.VMEM((2, wide, 1, SIDE), F32),
            pltpu.SemaphoreType.DMA((3,)),
            pltpu.SemaphoreType.DMA((2,)),
            pltpu.SemaphoreType.DMA((12,)),
            pltpu.SemaphoreType.DMA((12,)),
            pltpu.SemaphoreType.DMA((2, wide)),
            pltpu.SemaphoreType.DMA((2, wide)),
        ],
        compiler_params=pltpu.CompilerParams(
            collective_id=0, has_side_effects=True, vmem_limit_bytes=63 * 1024 * 1024
        ),
    )(
        images[:, 0],
        cotangent[:, 0],
        jnp.asarray(dft_constants()),
        pair_skip,
        patch_mask[:, 0],
        conv_weight,
        conv_bias,
    )
    grad, weight_grad, bias_grad = pl.pallas_call(
        deliver,
        grid=(2,),
        out_shape=(
            jax.ShapeDtypeStruct((2, 4, SIDE, SIDE), F32),
            jax.ShapeDtypeStruct((4, 9), F32),
            jax.ShapeDtypeStruct((1, 4), F32),
        ),
        in_specs=[member, vmem],
        out_specs=(member, vmem, vmem),
    )(grad, sums)
    return grad[:, None], weight_grad, bias_grad[0]


def solution(mesh):
    n_sec, n_tile = mesh.shape["sec"], mesh.shape["tile"]
    sizes = {64: (4, 2, 8), 4: (1, 2, 2)}.get(n_tile, (1, 1, n_tile))
    return jax.shard_map(
        functools.partial(on_device, (n_sec, *sizes)),
        mesh=mesh,
        in_specs=(
            P("sec", "tile", None, None),
            P("sec"),
            P("sec", "tile", None),
            P("sec", "tile", None, None, None),
            P(),
            P(),
        ),
        out_specs=(P("sec", "tile", None, None, None), P(), P()),
        check_vma=False,
    )
```

time: 59.2 us -> 47.8 us (0.81)
  Pallas kernels: 53 us -> 47 us
  local copies, waits for them, and re-layouts: 5.35 us -> 0 us
    pallas_call x1, Pallas kernels: 53 us -> 45.2 us  [on_device(): pl.pallas_call(functools.partial(kernel, shape), out_shape=(jax.ShapeDtyp...]
    unnamed x17 -> x0, local copies, waits for them, and re-layouts: 5.35 us -> none
    pallas_call x0 -> x1, Pallas kernels: none -> 1.78 us  [on_device(): pl.pallas_call(deliver, grid=(2,), out_shape=(jax.ShapeDtypeStruct((2, 4,...]
where the time goes in v1:
time: 47.8 us; the launch traced here: 47.7 us
  Pallas kernels  47 us (98%)
  between operations  0.64 us (1%)
    pallas_call x1, Pallas kernels, on_device(): pl.pallas_call(functools.partial(kernel, shape), out_shape=(jax.ShapeDtyp...  45.2 us
    pallas_call x1, Pallas kernels, on_device(): pl.pallas_call(deliver, grid=(2,), out_shape=(jax.ShapeDtypeStruct((2, 4,...  1.78 us

profile of v1, /device:TPU:1, one launch (start us, length us, event | category | flops | bytes accessed | tf_op | source)
XLA Modules:
  0.0 47.7 jit_solution(10671331424029204206)
XLA Ops:
  0.6 45.2 %shard_map.94 = (f32[2,4,128,128]{3,2,1,0:T(8,128)}, f32[1,128]{1,0:T(1,128)}) custom-call(bf16[2,128,128]{2,1,0:T(8,128)(2,1)} %bitcast.8, bf16[2,2,128,128]{3,2,1,0:T(8,128)(2,1)} %bitcast.7, bf16[4,256,256]{2,1,0:T(8,128)(2,1)} %constant.2.clone.tables_hbm, s32[2]{0:T(128)} %skip_ref.1, s32[2,2]{1,0:T(2,128)} %bitcast.9, f32[4,9]{1,0:T(4,128)} %weight_ref.1, ...), custom_call_target="tpu_custom_call" | custom-call | tf_op jit(solution)/shard_map/pallas_call | solution.py:485
  45.9 1.8 %shard_map.95 = (f32[2,4,128,128]{3,2,1,0:T(8,128)}, f32[4,9]{1,0:T(4,128)}, f32[1,4]{1,0:T(1,128)}) custom-call(f32[2,4,128,128]{3,2,1,0:T(8,128)} %get-tuple-element.8.grad_ref, f32[1,128]{1,0:T(1,128)} %get-tuple-element.9.sums_ref), custom_call_target="tpu_custom_call" | custom-call | tf_op jit(solution)/shard_map/pallas_call | solution.py:530

commit v2 on v1

--- a/solution.py
+++ b/solution.py
@@ -89,8 +89,8 @@
     n_tile = n_x * n_z * n_y
     sec = lax.axis_index("sec")
     tile = lax.axis_index("tile")
-    at_x = tile // (n_z * n_y)
-    at_z = lax.rem(tile // n_y, n_z)
+    at_x = lax.div(tile, n_z * n_y)
+    at_z = lax.rem(lax.div(tile, n_y), n_z)
     at_y = lax.rem(tile, n_y)
 
     def sec_at(step):
@@ -99,26 +99,36 @@
     def tile_at(step):
         return lax.rem(tile + (step + n_tile), n_tile)
 
-    around = [(1, 0), (-1, 0), (0, 1), (0, -1)]
-    spots = (sec * n_z + at_z, at_x * n_y + at_y)
-    sizes = (n_sec * n_z, n_x * n_y)
-
-    def in_ring(stage, step):
-        there = lax.rem(spots[stage] + step, sizes[stage])
-        if stage == 0:
-            return there // n_z, (at_x * n_z + lax.rem(there, n_z)) * n_y + at_y
-        return sec, (there // n_y * n_z + at_z) * n_y + lax.rem(there, n_y)
-
-    rings = [[in_ring(stage, d) for d in range(1, sizes[stage])] for stage in range(2)]
+    near = sec + 1 - 2 * lax.rem(sec, 2)
+    far = lax.rem(sec - 1 + 2 * lax.rem(sec, 2) + n_sec, n_sec)
+    around = [(sec, tile_at(1)), (sec, tile_at(-1)), (far, tile), (near, tile)]
+    deep = n_sec // 2 * n_z
+    at_deep = lax.div(sec, 2) * n_z + at_z
+    core = lax.rem(sec, 2)
+    spots = (at_deep * 2 + core, at_x * n_y + at_y)
+
+    def hops(step, size):
+        return min(step, size - step)
+
+    def in_line(step):
+        there = lax.rem(at_deep + step[0], deep)
+        other = lax.rem(core + step[1], 2)
+        device = (lax.div(there, n_z) * 2 + other, (at_x * n_z + lax.rem(there, n_z)) * n_y + at_y)
+        return device
+
+    def in_plane(step):
+        to_x, to_y = lax.rem(at_x + step[0], n_x), lax.rem(at_y + step[1], n_y)
+        return sec, (to_x * n_z + at_z) * n_y + to_y
+
+    line = [(i, j) for i in range(deep) for j in range(2)][1:]
+    plane = [(i, j) for i in range(n_x) for j in range(n_y)][1:]
+    line.sort(key=lambda step: -hops(step[0], deep))
+    plane.sort(key=lambda step: -hops(step[0], n_x) - hops(step[1], n_y))
+    rings = [[in_line(step) for step in line], [in_plane(step) for step in plane]]
+    sizes = (deep * 2, n_x * n_y)
     barrier = pltpu.get_barrier_semaphore()
-    for a, b in around:
-        pl.semaphore_signal(
-            barrier, inc=1, device_id=(sec_at(a), tile_at(b)), device_id_type=MESH
-        )
-    for group in rings:
-        for device in group:
-            pl.semaphore_signal(barrier, inc=1, device_id=device, device_id_type=MESH)
-
+    for device in around:
+        pl.semaphore_signal(barrier, inc=1, device_id=device, device_id_type=MESH)
     middle = pl.ds(STEP, SIDE)
     loads = [
         pltpu.make_async_copy(images_hbm, imgs.at[1, :, middle], in_sem.at[0]),
@@ -127,6 +137,9 @@
     ]
     for load in loads:
         load.start()
+    for group in rings[::-1]:
+        for device in group:
+            pl.semaphore_signal(barrier, inc=1, device_id=device, device_id_type=MESH)
     pl.semaphore_wait(barrier, len(around) + sum(len(g) for g in rings))
 
     copies = {}
@@ -150,8 +163,10 @@
     bottom = pl.ds(SIDE + STEP, EXT - SIDE - STEP)
     send("down0", down, imgs.at[1, :, top], (sec, tile_at(1)))
     send("up0", up, imgs.at[1, :, bottom], (sec, tile_at(-1)))
-    for a in (1, -1):
-        send(("mid", a), images_hbm, imgs.at[1 - a, :, middle], (sec_at(a), tile))
+    near_slot = 2 * core
+    far_slot = 2 - near_slot
+    for side, to, slot in (("near", near, near_slot), ("far", far, far_slot)):
+        send((side, "mid"), images_hbm, imgs.at[slot, :, middle], (to, tile))
 
     skip_even = skip_ref[0]
     skip_odd = skip_ref[1]
@@ -288,103 +303,114 @@
     lax.fori_loop(0, 3, band_rows, 0)
     loads[2].wait()
     loads[0].wait()
-    def own_cots(index, carry):
+    def own_cots(index):
         cot_pair(1, index + 1)
-        return carry
-
-    lax.fori_loop(0, 2, own_cots, 0)
+
+    for index in range(2):
+        own_cots(index)
     gacc[...] = jnp.zeros_like(gacc)
     acc[...] = jnp.zeros_like(acc)
-    for name in ("down0", "up0", "cot_t"):
+    for name in ("down0", "up0"):
         copies[name].wait_recv()
-
-    @pl.when(first_tile)
-    def _():
-        cots[1, 0] = jnp.zeros((2, SIDE, SIDE), BF16)
 
     @pl.when(last_tile)
     def _():
         imgs[1, :, bottom] = jnp.zeros((2, EXT - SIDE - STEP, SIDE), BF16)
 
-    for a in (1, -1):
+    for side, to, slot in (("near", near, near_slot), ("far", far, far_slot)):
         for name, rows in (("down", top), ("up", bottom)):
-            send((name, a), imgs.at[1, :, rows], imgs.at[1 - a, :, rows], (sec_at(a), tile))
-    send("cot_d", cots.at[1, 0], cots.at[0, 0], (sec_at(1), tile))
-
-    def own_sections(member, carry):
+            send((side, name), imgs.at[1, :, rows], imgs.at[slot, :, rows], (to, tile))
+    def own_sections(member):
         image = imgs[1, member].astype(F32)
         shifts[member, 0] = image
         shifts[member, 1] = pltpu.roll(image, SIDE - 1, 1) * in_one
         shifts[member, 2] = pltpu.roll(image, SIDE - 2, 1) * in_two
         encode(member, shifts.at[member, 0])
-        return carry
-
-    lax.fori_loop(0, 2, own_sections, 0)
+
+    for index in range(2):
+        own_sections(index)
+    copies["cot_t"].wait_recv()
+
+    @pl.when(first_tile)
+    def _():
+        cots[1, 0] = jnp.zeros((2, SIDE, SIDE), BF16)
+
+    send("cot_d", cots.at[1, 0], cots.at[0, 0], (sec_at(1), tile))
     cot_pair(1, 0)
 
-    def own_spectra(anchor, carry):
+    def own_spectra(anchor):
         k_re, k_im = kernel_of(1, anchor, 0)
         re, im = plain_product(k_re, k_im, spectrum(0, anchor))
         gspec[anchor, 0:SIDE] = even_next * re
         gspec[anchor, SIDE:] = even_next * im
-        return carry
-
-    lax.fori_loop(0, 3, own_spectra, 0)
-
-    def wait_images(a):
-        for name in ("mid", "down", "up"):
-            copies[name, a].wait_recv()
-
-    def step(phase, carry):
+
+    for index in range(3):
+        own_spectra(index)
+
+    def step(phase):
+        for name in ("mid", "up", "down"):
+            copies[("near", "far")[phase], name].wait_recv()
+        base = 2 * phase
         before = lax.rem(sec + phase, 2) == 1
 
         @pl.when(before)
         def _():
-            wait_images(1)
-            pixels[0] = imgs[0, 0].astype(F32)
-            pixels[1] = imgs[0, 1].astype(F32)
+            pixels[base] = imgs[0, 0].astype(F32)
+            pixels[base + 1] = imgs[0, 1].astype(F32)
 
         @pl.when(jnp.logical_not(before))
         def _():
-            wait_images(-1)
             ahead = imgs[2, 0].astype(F32)
-            pixels[2] = even_next * shifts[1, 0] + (1.0 - even_next) * ahead
-            pixels[3] = odd_next * ahead + (1.0 - odd_next) * imgs[2, 1].astype(F32)
-
-        base = 2 * lax.rem(sec + phase + 1, 2)
+            pixels[base] = even_next * shifts[1, 0] + (1.0 - even_next) * ahead
+            pixels[base + 1] = odd_next * ahead + (1.0 - odd_next) * imgs[2, 1].astype(F32)
+
         for i in range(2):
             encode(2 + base + i, pixels.at[base + i])
         for anchor in range(3):
             for i in range(2):
                 aspec[base + i, anchor] = spectrum(2 + base + i, anchor)
-        return carry
-
-    lax.fori_loop(0, 2, step, 0)
-
-    for name in ("flag", "cot_s", "cot_d"):
+
+    step(0)
+    for name in ("flag", "cot_s"):
         copies[name].wait_recv()
 
     @pl.when(sec == 0)
     def _():
-        cots[0] = jnp.zeros((3, 2, SIDE, SIDE), BF16)
+        cots[0, 1:3] = jnp.zeros((2, 2, SIDE, SIDE), BF16)
+
+    def prior_cots(index):
+        cot_pair(0, index + 1)
+
+    for index in range(2):
+        prior_cots(index)
+    step(1)
+    copies["cot_d"].wait_recv()
+
+    @pl.when(sec == 0)
+    def _():
+        cots[0, 0] = jnp.zeros((2, SIDE, SIDE), BF16)
+
+    cot_pair(0, 0)
+
+    prior = 2 - 2 * core
+    later = 2 * core
 
     def finish(anchor):
-        cot_pair(0, anchor)
         came_next = flag_in[0:1, 0:1]
         came_after = flag_in[1:2, 0:1]
         k_re, k_im = kernel_of(0, anchor, 1)
-        last_re, last_im = plain_product(k_re, k_im, aspec[1, anchor])
+        last_re, last_im = plain_product(k_re, k_im, aspec[prior + 1, anchor])
         k_re, k_im = kernel_of(0, anchor, 0)
-        p_re, p_im = plain_product(came_after * k_re, came_after * k_im, aspec[0, anchor])
+        p_re, p_im = plain_product(came_after * k_re, came_after * k_im, aspec[prior, anchor])
         g_re = p_re + came_next * last_re
         g_im = p_im + came_next * last_im
         h_re = gspec[anchor, 0:SIDE] + (1.0 - came_next) * last_re
         h_im = gspec[anchor, SIDE:] + (1.0 - came_next) * last_im
         k_re, k_im = kernel_of(1, anchor, 0)
-        p_re, p_im = conj_product(k_re, k_im, aspec[2, anchor])
+        p_re, p_im = conj_product(k_re, k_im, aspec[later, anchor])
         g_re, g_im = g_re + p_re, g_im + p_im
         k_re, k_im = kernel_of(1, anchor, 1)
-        p_re, p_im = conj_product(k_re, k_im, aspec[3, anchor])
+        p_re, p_im = conj_product(k_re, k_im, aspec[later + 1, anchor])
         h_re, h_im = h_re + p_re, h_im + p_im
         for member, (re, im) in enumerate(((g_re, g_im), (h_re, h_im))):
             half = left_dot(w_high(), w_low(), jnp.concatenate([re, im], axis=0))
@@ -398,21 +424,8 @@
                 start = anchor * STEP
                 gacc[member, c, pl.ds(start, SIDE), :] += scale * (slope - unit * along)
 
-    for anchor in range(3):
-        finish(anchor)
-
-    results = [
-        pltpu.make_async_copy(
-            gacc.at[member, :, middle], grad_out.at[member], out_sem.at[member]
-        )
-        for member in range(2)
-    ]
-    for result in results:
-        result.start()
-
-    def weight_steps(index, carry):
-        member = index // 2
-        start = pl.multiple_of(STEP + lax.rem(index, 2) * STEP, STEP)
+    def weight_steps(member, half):
+        start = STEP + half * STEP
         slopes = []
         for c in range(4):
             values = feat[member, c, pl.ds(start, STEP), :]
@@ -425,9 +438,23 @@
                 for c in range(4):
                     part = slopes[c] * shifted
                     acc[10 * c + 3 * u + v] += jnp.sum(part.reshape(STEP // 8, 8, SIDE), axis=0)
-        return carry
-
-    lax.fori_loop(0, 4, weight_steps, 0)
+
+    finish(0)
+    finish(1)
+    weight_steps(0, 0)
+    weight_steps(1, 0)
+    finish(2)
+    results = [
+        pltpu.make_async_copy(
+            gacc.at[member, :, middle], grad_out.at[member], out_sem.at[member]
+        )
+        for member in range(2)
+    ]
+    for result in results:
+        result.start()
+
+    weight_steps(0, 1)
+    weight_steps(1, 1)
     place = lax.broadcasted_iota(jnp.int32, (1, SIDE), 1)
     mine = jnp.zeros((1, SIDE), F32)
     for index in range(40):

time: 47.8 us -> 45.8 us (0.958)
  Pallas kernels: 47 us -> 45 us
    pallas_call x1, Pallas kernels: 45.2 us -> 43.2 us  [on_device(): pl.pallas_call(functools.partial(kernel, shape), out_shape=(jax.ShapeDtyp...]
where the time goes in v2:
time: 45.8 us; the launch traced here: 45.6 us
  Pallas kernels  45 us (98%)
  between operations  0.64 us (1%)
    pallas_call x1, Pallas kernels, on_device(): pl.pallas_call(functools.partial(kernel, shape), out_shape=(jax.ShapeDtyp...  43.2 us
    pallas_call x1, Pallas kernels, on_device(): pl.pallas_call(deliver, grid=(2,), out_shape=(jax.ShapeDtypeStruct((2, 4,...  1.78 us

profile of v2, /device:TPU:1, one launch (start us, length us, event | category | flops | bytes accessed | tf_op | source)
XLA Modules:
  0.0 45.6 jit_solution(4398825490748574516)
XLA Ops:
  0.6 43.2 %shard_map.94 = (f32[2,4,128,128]{3,2,1,0:T(8,128)}, f32[1,128]{1,0:T(1,128)}) custom-call(bf16[2,128,128]{2,1,0:T(8,128)(2,1)} %bitcast.8, bf16[2,2,128,128]{3,2,1,0:T(8,128)(2,1)} %bitcast.7, bf16[4,256,256]{2,1,0:T(8,128)(2,1)} %constant.2.clone.tables_hbm, s32[2]{0:T(128)} %skip_ref.1, s32[2,2]{1,0:T(2,128)} %bitcast.9, f32[4,9]{1,0:T(4,128)} %weight_ref.1, ...), custom_call_target="tpu_custom_call" | custom-call | tf_op jit(solution)/shard_map/pallas_call | solution.py:512
  43.9 1.8 %shard_map.95 = (f32[2,4,128,128]{3,2,1,0:T(8,128)}, f32[4,9]{1,0:T(4,128)}, f32[1,4]{1,0:T(1,128)}) custom-call(f32[2,4,128,128]{3,2,1,0:T(8,128)} %get-tuple-element.8.grad_ref, f32[1,128]{1,0:T(1,128)} %get-tuple-element.9.sums_ref), custom_call_target="tpu_custom_call" | custom-call | tf_op jit(solution)/shard_map/pallas_call | solution.py:557

commit v3 on v2

--- a/solution.py
+++ b/solution.py
@@ -55,12 +55,16 @@
     images_hbm,
     cot_hbm,
     tables_hbm,
+    skip_hbm,
+    mask_hbm,
+    weight_hbm,
+    bias_hbm,
+    grad_out,
+    sums_out,
     skip_ref,
     mask_ref,
     weight_ref,
     bias_ref,
-    grad_out,
-    sums_out,
     own_cot,
     tables,
     imgs,
@@ -134,6 +138,10 @@
         pltpu.make_async_copy(images_hbm, imgs.at[1, :, middle], in_sem.at[0]),
         pltpu.make_async_copy(cot_hbm, own_cot, in_sem.at[1]),
         pltpu.make_async_copy(tables_hbm, tables, in_sem.at[2]),
+        pltpu.make_async_copy(skip_hbm, skip_ref, in_sem.at[3]),
+        pltpu.make_async_copy(mask_hbm, mask_ref, in_sem.at[4]),
+        pltpu.make_async_copy(weight_hbm, weight_ref, in_sem.at[5]),
+        pltpu.make_async_copy(bias_hbm, bias_ref, in_sem.at[6]),
     ]
     for load in loads:
         load.start()
@@ -168,6 +176,8 @@
     for side, to, slot in (("near", near, near_slot), ("far", far, far_slot)):
         send((side, "mid"), images_hbm, imgs.at[slot, :, middle], (to, tile))
 
+    for load in loads[3:]:
+        load.wait()
     skip_even = skip_ref[0]
     skip_odd = skip_ref[1]
     even_next = jnp.where(skip_even == 1, 1.0, 0.0).astype(F32)
@@ -504,7 +514,6 @@
 
 def on_device(shape, images, pair_skip, patch_mask, cotangent, conv_weight, conv_bias):
     hbm = pl.BlockSpec(memory_space=pl.ANY)
-    smem = pl.BlockSpec(memory_space=pltpu.SMEM)
     vmem = pl.BlockSpec(memory_space=pltpu.VMEM)
     wide = max(shape[0] * shape[2], shape[1] * shape[3])
     held = pl.BlockSpec(memory_space=pltpu.HBM)
@@ -515,9 +524,13 @@
             jax.ShapeDtypeStruct((2, 4, SIDE, SIDE), F32),
             jax.ShapeDtypeStruct((1, SIDE), F32),
         ),
-        in_specs=[held, held, held, smem, smem, smem, smem],
+        in_specs=[held] * 7,
         out_specs=(hbm, vmem),
         scratch_shapes=[
+            pltpu.SMEM((2,), jnp.int32),
+            pltpu.SMEM((2, 2), jnp.int32),
+            pltpu.SMEM((4, 9), F32),
+            pltpu.SMEM((4,), F32),
             pltpu.VMEM((2, 2, SIDE, SIDE), BF16),
             pltpu.VMEM((4, 2 * SIDE, 2 * SIDE), BF16),
             pltpu.VMEM((3, 2, EXT, SIDE), BF16),
@@ -535,7 +548,7 @@
             pltpu.VMEM((2, 4, 4 * STEP, SIDE), F32),
             pltpu.VMEM((40, 8, SIDE), F32),
             pltpu.VMEM((2, wide, 1, SIDE), F32),
-            pltpu.SemaphoreType.DMA((3,)),
+            pltpu.SemaphoreType.DMA((7,)),
             pltpu.SemaphoreType.DMA((2,)),
             pltpu.SemaphoreType.DMA((12,)),
             pltpu.SemaphoreType.DMA((12,)),

time: 45.8 us -> 45.1 us (0.985)
  Pallas kernels: 45 us -> 44.3 us
    pallas_call x1, Pallas kernels: 43.2 us -> 42.5 us  [on_device(): pl.pallas_call(functools.partial(kernel, shape), out_shape=(jax.ShapeDtyp...]
where the time goes in v3:
time: 45.1 us; the launch traced here: 45 us
  Pallas kernels  44.3 us (98%)
  between operations  0.64 us (1%)
    pallas_call x1, Pallas kernels, on_device(): pl.pallas_call(functools.partial(kernel, shape), out_shape=(jax.ShapeDtyp...  42.5 us
    pallas_call x1, Pallas kernels, on_device(): pl.pallas_call(deliver, grid=(2,), out_shape=(jax.ShapeDtypeStruct((2, 4,...  1.78 us

profile of v3, /device:TPU:1, one launch (start us, length us, event | category | flops | bytes accessed | tf_op | source)
XLA Modules:
  0.0 45.0 jit_solution(11139582585666725677)
XLA Ops:
  0.6 42.5 %shard_map.94 = (f32[2,4,128,128]{3,2,1,0:T(8,128)}, f32[1,128]{1,0:T(1,128)}) custom-call(bf16[2,128,128]{2,1,0:T(8,128)(2,1)} %bitcast.8, bf16[2,2,128,128]{3,2,1,0:T(8,128)(2,1)} %bitcast.7, bf16[4,256,256]{2,1,0:T(8,128)(2,1)} %constant.2.clone.tables_hbm, s32[2]{0:T(128)} %skip_hbm.1, s32[2,2]{1,0:T(2,128)} %bitcast.9, f32[4,9]{1,0:T(4,128)} %weight_hbm.1, ...), custom_call_target="tpu_custom_call" | custom-call | tf_op jit(solution)/shard_map/pallas_call | solution.py:521
  43.2 1.8 %shard_map.95 = (f32[2,4,128,128]{3,2,1,0:T(8,128)}, f32[4,9]{1,0:T(4,128)}, f32[1,4]{1,0:T(1,128)}) custom-call(f32[2,4,128,128]{3,2,1,0:T(8,128)} %get-tuple-element.8.grad_ref, f32[1,128]{1,0:T(1,128)} %get-tuple-element.9.sums_ref), custom_call_target="tpu_custom_call" | custom-call | tf_op jit(solution)/shard_map/pallas_call | solution.py:570
